TPU v7x, 32 devices: a whole 2x2x4 slice. The times are simulated.
32 devices in a mesh: ctx: 8 (over z, y), head: 4 (over x, core).
Axes of the slice: x: 2, y: 2, z: 4, core: 2. Of those that a mesh axis runs over, the one named last changes fastest.
Arguments:
- ctx_queries: bfloat16 [8192, 4096], P('ctx', 'head'), may hold values from -8 to 8
- ctx_keys: bfloat16 [8192, 512], P('ctx', 'head'), may hold values from -12 to 12
- ctx_values: bfloat16 [8192, 512], P('ctx', 'head'), may hold values from -12 to 12
- new_queries: bfloat16 [64, 4096], P('ctx', 'head'), may hold values from -8 to 8
- out_weight: bfloat16 [4096, 8192], P('head', 'ctx'), may hold values from -0.09375 to 0.09375
- host_block: int32 [8], replicated, may hold values from 0 to 7, each once
- block_lengths: int32 [8], replicated, may hold values from 256 to 1024, as said below
Outputs:
- context_out: bfloat16 [8192, 4096], P('ctx', 'head')
- answer: bfloat16 [64, 8192], P('head', 'ctx')
Inputs may be any that keep to these rules, and one draw needn't show every extreme that they name: `block_lengths`: some block has 1024 valid tokens and another exactly 256. `host_block`: a permutation of the blocks.
All inputs are finite; a program needn't handle non-finite values.
Results may differ from a plain program's by a relative error of at most 0.002.
The roundings to bfloat16 on the way count: a program that leaves them out, or rounds other values in their place, can miss the bound.
Values may be sent and summed in bfloat16 or wider, within the bound.
No kernel may reach another device: no remote copies, remote signals or barrier semaphores. Data moves between devices by JAX's collectives and lax.ppermute only.
A program may use at most 128 MiB of HBM per device.

v0:
```python
import jax
import jax.numpy as jnp
from jax import lax
from jax.sharding import PartitionSpec as P

HD = 128
GROUP = 8
KV_DEV = 1
BLOCK = 1024


NEG = -1e30
CLIP_FACTOR = 2.0


def from_root(x, axis, root):
    mine = lax.axis_index(axis) == root
    return lax.psum(jnp.where(mine, x, jnp.zeros_like(x)), axis)


def joined(part, axis, combine):
    gathered = jax.tree.map(lambda a: lax.all_gather(a, axis), part)

    def take(source):
        return jax.tree.map(lambda a: lax.dynamic_index_in_dim(a, source, 0, False), gathered)

    return lax.fori_loop(
        1, lax.axis_size(axis), lambda source, state: combine(state, take(source)), take(0)
    )


def sign_matrix(size):
    positions = jnp.arange(size, dtype=jnp.int32)
    common = jnp.bitwise_and(positions[:, None], positions[None, :])
    parity = jnp.zeros((size, size), jnp.int32)
    for bit_number in range(int(size).bit_length()):
        parity = parity + jnp.bitwise_and(jnp.right_shift(common, bit_number), 1)
    parity = parity % 2
    return (1 - 2 * parity).astype(jnp.bfloat16)


def rotate(matrix, sign_table):
    head_width = matrix.shape[-1]
    return (
        jnp.dot(matrix, sign_table, preferred_element_type=jnp.float32) * head_width ** (-0.5)
    ).astype(jnp.bfloat16)


def store_rotated(matrix, sign_table):
    head_width = matrix.shape[-1]
    turned = jnp.dot(matrix, sign_table, preferred_element_type=jnp.float32) * head_width ** (-0.5)
    ceiling = CLIP_FACTOR * jnp.sqrt(jnp.mean(turned * turned, axis=-1, keepdims=True))
    return jnp.clip(turned, -ceiling, ceiling).astype(jnp.bfloat16)


def block_attention(
    queries, own_keys, own_values, anchor_keys, anchor_values, own_len, anchor_len, is_anchor
):
    row_count = queries.shape[1]
    head_width = queries.shape[2]
    positions = jnp.arange(row_count, dtype=jnp.int32)
    anchor_ok = jnp.logical_and(positions < anchor_len, jnp.logical_not(is_anchor))
    own_ok = jnp.logical_and(positions[None, :] <= positions[:, None], positions[None, :] < own_len)
    allowed = jnp.concatenate(
        [jnp.broadcast_to(anchor_ok[None, :], (row_count, row_count)), own_ok], axis=1
    )
    all_keys = jnp.concatenate([anchor_keys, own_keys], axis=0)
    all_values = jnp.concatenate([anchor_values, own_values], axis=0)

    def block_single_head(query_rows):
        scores = jnp.dot(
            query_rows, all_keys.T, preferred_element_type=jnp.float32
        ) * head_width ** (-0.5)
        scores = jnp.where(allowed, scores, NEG)
        row_max = jnp.max(scores, axis=1, keepdims=True)
        powers = jnp.where(allowed, jnp.exp(scores - row_max), 0.0)
        weights = powers.astype(jnp.bfloat16)
        totals = jnp.sum(powers, axis=1)
        output = jnp.dot(weights, all_values, preferred_element_type=jnp.float32) / totals[:, None]
        return jnp.where((positions < own_len)[:, None], output, 0.0).astype(jnp.bfloat16)

    return lax.map(block_single_head, queries)


def host_partial(queries, rot_keys, rot_values, own_len):
    head_width = queries.shape[2]
    usable = jnp.arange(rot_keys.shape[0], dtype=jnp.int32) < own_len

    def host_single_head(query_rows):
        scores = jnp.dot(
            query_rows, rot_keys.T, preferred_element_type=jnp.float32
        ) * head_width ** (-0.5)
        scores = jnp.where(usable[None, :], scores, NEG)
        row_max = jnp.max(scores, axis=1)
        powers = jnp.where(usable[None, :], jnp.exp(scores - row_max[:, None]), 0.0)
        weights = powers.astype(jnp.bfloat16)
        return (
            row_max,
            jnp.sum(powers, axis=1),
            jnp.dot(weights, rot_values, preferred_element_type=jnp.float32),
        )

    return lax.map(host_single_head, queries)


def finish(output, totals, sign_table):
    head_width = output.shape[2]
    scaled = output / totals[..., None]
    turned = jnp.einsum(
        "hrd,de->rhe", scaled, sign_table.astype(jnp.float32), precision=lax.Precision.HIGHEST
    )
    turned = turned * head_width ** (-0.5)
    return turned.reshape(output.shape[1], -1).astype(jnp.bfloat16)


def merge_pair(first, second):
    overall = jnp.maximum(first[0], second[0])
    first_factor = jnp.exp(first[0] - overall)
    second_factor = jnp.exp(second[0] - overall)
    return (
        overall,
        first[1] * first_factor + second[1] * second_factor,
        first[2] * first_factor[..., None] + second[2] * second_factor[..., None],
    )


def per_device(
    ctx_queries, ctx_keys, ctx_values, new_queries, out_weight, host_block, block_lengths
):
    sign_table = sign_matrix(HD)
    host_count = lax.axis_size("ctx")
    self_host = lax.axis_index("ctx")
    host_ids = jnp.arange(host_count, dtype=jnp.int32)
    block_ids = jnp.arange(block_lengths.shape[0], dtype=jnp.int32)
    own_block = jnp.sum(jnp.where(host_ids == self_host, host_block, 0))
    own_len = jnp.sum(jnp.where(block_ids == own_block, block_lengths, 0))
    anchor_host = jnp.sum(jnp.where(host_block == 0, host_ids, 0))
    anchor_len = block_lengths[0]
    is_anchor = own_block == 0
    key_value = jnp.stack([ctx_keys, ctx_values])
    anchor = from_root(key_value, "ctx", anchor_host)
    query_grid = ctx_queries.reshape(BLOCK, KV_DEV, GROUP, HD)
    key_grid = ctx_keys.reshape(BLOCK, KV_DEV, HD)
    value_grid = ctx_values.reshape(BLOCK, KV_DEV, HD)
    anchor_k = anchor[0].reshape(BLOCK, KV_DEV, HD)
    anchor_v = anchor[1].reshape(BLOCK, KV_DEV, HD)

    def each_group(group_index):
        return block_attention(
            query_grid[:, group_index].transpose(1, 0, 2),
            key_grid[:, group_index],
            value_grid[:, group_index],
            anchor_k[:, group_index],
            anchor_v[:, group_index],
            own_len,
            anchor_len,
            is_anchor,
        )

    outputs = lax.map(each_group, jnp.arange(KV_DEV, dtype=jnp.int32))
    context_out = outputs.transpose(2, 0, 1, 3).reshape(BLOCK, KV_DEV * GROUP * HD)
    gathered = lax.all_gather(new_queries, "ctx", axis=0, tiled=True)
    query_count = gathered.shape[0]
    gathered_grid = gathered.reshape(query_count, KV_DEV, GROUP, HD)

    def each_group_query(group_index):
        query_rot = rotate(
            gathered_grid[:, group_index].reshape(query_count * GROUP, HD), sign_table
        )
        query_rot = query_rot.reshape(query_count, GROUP, HD).transpose(1, 0, 2)
        key_store = store_rotated(key_grid[:, group_index], sign_table)
        value_store = store_rotated(value_grid[:, group_index], sign_table)
        return host_partial(query_rot, key_store, value_store, own_len)

    maxima, sums, partial_out = lax.map(each_group_query, jnp.arange(KV_DEV, dtype=jnp.int32))
    maxima = maxima.reshape(KV_DEV * GROUP, query_count)
    sums = sums.reshape(KV_DEV * GROUP, query_count)
    partial_out = partial_out.reshape(KV_DEV * GROUP, query_count, HD)
    overall, totals, merged = joined((maxima, sums, partial_out), "ctx", merge_pair)
    attended = finish(merged, totals, sign_table)
    answer = lax.psum_scatter(
        jnp.dot(attended, out_weight, preferred_element_type=jnp.float32),
        "head",
        scatter_dimension=0,
        tiled=True,
    ).astype(jnp.bfloat16)
    return (context_out, answer)


def solution(mesh):
    placed = (
        P("ctx", "head"),
        P("ctx", "head"),
        P("ctx", "head"),
        P("ctx", "head"),
        P("head", "ctx"),
        P(),
        P(),
    )
    return jax.shard_map(
        per_device,
        mesh=mesh,
        in_specs=placed,
        out_specs=(P("ctx", "head"), P("head", "ctx")),
        check_vma=False,
    )
```

profile of v0, /device:TPU:0, one launch (start us, length us, event | category | flops | bytes accessed | tf_op | source)
XLA Modules:
  0.0 250.6 jit_solution(14056757116501099829)
XLA Ops:
  7.3 1.5 fusion.70
  9.4 1.9 maximum_select_fusion
  11.4 1.3 multiply_reduce_fusion.1
  13.1 32.5 %all_gather.12 = bf16[64,1024]{1,0:T(8,128)(2,1)S(1)} all-gather(bf16[8,1024]{1,0:T(8,128)(2,1)S(1)} %copy-done.5), channel_id=1, replica_groups=mesh['ctx'=8,'head'=4] {'ctx'}, dimensions={0}, use_global_device_ids=true | all-gather | bytes 147456 | tf_op jit(solution)/shard_map/all_gather | solution.py:162
  46.6 1.4 fusion.69
  48.0 17.0 %while.65 = (s32[]{:T(128)}, f32[8,64]{1,0:T(8,128)S(1)}, f32[8,64]{1,0:T(8,128)S(1)}, f32[8,64,128]{2,1,0:T(8,128)}, bf16[8,64,128]{2,1,0:T(8,128)(2,1)S(1)}, /...) while((s32[]{:T(128)}, f32[8,64]{1,0:T(8,128)S(1)}, ...), condition=%wide.region_13.14_spmd.clone, body=%wide.region_10.13_spmd.clone.sunk | while | flops 34145152 | bytes 1366145 | solution.py:103
  65.7 4.0 %copy.21 = bf16[1024,1024]{0,1:T(8,128)(2,1)} copy(bf16[1024,1024]{1,0:T(8,128)(2,1)} %param.13) | data formatting | bytes 4194304 | tf_op args[0]
  69.7 30.5 %all-gather = f32[64,64]{1,0:T(8,128)S(1)} all-gather(f32[8,64]{1,0:T(8,128)S(1)} %get-tuple-element.323), channel_id=2, replica_groups=mesh['ctx'=8,'head'=4] {'ctx'}, dimensions={0}, use_global_device_ids=true | all-gather | bytes 18432 | tf_op jit(solution)/shard_map/all_gather | solution.py:22
  100.2 30.7 %all-gather.1 = f32[64,64]{1,0:T(8,128)S(1)} all-gather(f32[8,64]{1,0:T(8,128)S(1)} %get-tuple-element.324), channel_id=3, replica_groups=mesh['ctx'=8,'head'=4] {'ctx'}, dimensions={0}, use_global_device_ids=true | all-gather | bytes 18432 | tf_op jit(solution)/shard_map/all_gather | solution.py:22
  131.9 2.4 pad_add_fusion
  136.3 1.6 all-gather.5.cloned.1.call-done
  138.8 8.8 %while.63 = (s32[]{:T(128)}, f32[8,64]{1,0:T(8,128)S(1)}, f32[8,64]{1,0:T(8,128)S(1)}, f32[8,64,128]{2,1,0:T(8,128)S(1)}, f32[8,8,64]{2,1,0:T(8,128)S(1)}, /*ind...) while((s32[]{:T(128)}, f32[8,64]{1,0:T(8,128)S(1)}, ...), condition=%wide.region_15.16_spmd, body=%wide.region_14.15_spmd.sunk | while | flops 199685 | bytes 807063 | solution.py:27
  138.9 1.2 fusion.130
  140.1 1.2 fusion.130
  141.4 1.2 fusion.130
  142.7 1.2 fusion.130
  143.9 1.2 fusion.130
  145.2 1.2 fusion.130
  146.4 1.2 fusion.130
  148.0 1.2 fusion.54
  149.3 88.4 %while.64 = (s32[]{:T(128)}, bf16[8,1024,128]{2,1,0:T(8,128)(2,1)}, s32[]{:T(128)}, bf16[8,1024,128]{1,2,0:T(8,128)(2,1)}, bf16[2048,128]{1,0:T(8,128)(2,1)S(1)}...) while((s32[]{:T(128)}, bf16[8,1024,128]{2,1,0:T(8,128)(2,1)}, ...), condition=%wide.region_7.8_spmd.clone, body=%wide.region_4.7_spmd.clone.sunk | while | flops 1101396992 | bytes 41441412 | solution.py:82
  149.3 3.8 %fusion.134 = (f32[1024]{0:T(1024)S(1)}, f32[1024,2048]{1,0:T(8,128)S(1)}) fusion(pred[1024,2048]{1,0:T(32,128)(4,1)} %get-tuple-element.643, bf16[2048,128]{1,0:T(8,128)(2,1)S(1)} %get-tuple-element.642, bf16[8,1024,128]{1,2,0:T(8,128)(2,1)} %get-tuple-element.641, s32[]{:T(128)S(6)} %copy.45), kind=kOutput, calls=%fused_computation.12.clone.1 | convolution fusion | flops 543161344 | bytes 11276292 | tf_op jit(solution)/shard_map/while/body/eval_jaxpr/while/body/eval_jaxpr/dot_general | solution.py:71
  153.1 3.0 %fusion.135 = f32[1024]{0:T(1024)S(1)} fusion(pred[1024,2048]{1,0:T(32,128)(4,1)S(1)} %copy-done.1, f32[1024,2048]{1,0:T(8,128)S(1)} %get-tuple-element.610, f32[1024]{0:T(1024)S(1)} %get-tuple-element.611), kind=kLoop, calls=%fused_computation.13.clone.1 | loop fusion | flops 10484736 | bytes 10493952 | tf_op jit(solution)/shard_map/while/body/eval_jaxpr/while/body/eval_jaxpr/reduce_sum | solution.py:78
  156.8 3.5 %fusion.136 = bf16[8,1024,128]{2,1,0:T(8,128)(2,1)} fusion(bf16[8,1024,128]{2,1,0:T(8,128)(2,1)} %get-tuple-element.631, s32[]{:T(128)S(6)} %copy.45, bf16[2048,128]{1,0:T(8,128)(2,1)S(1)} %get-tuple-element.644, pred[1024,2048]{1,0:T(32,128)(4,1)S(1)} %copy-done.1, f32[1024,2048]{1,0:T(8,128)S(1)} %get-tuple-element.610, ...), kind=kOutput, calls=%fused_computation.20.clone.1 | convolution fusion | flops 547749888 | bytes 11281412 | tf_op jit(solution)/shard_map/while/body/eval_jaxpr/while/body/eval_jaxpr/dot_general | solution.py:79
  160.3 3.8 %fusion.134 = (f32[1024]{0:T(1024)S(1)}, f32[1024,2048]{1,0:T(8,128)S(1)}) fusion(pred[1024,2048]{1,0:T(32,128)(4,1)} %get-tuple-element.643, bf16[2048,128]{1,0:T(8,128)(2,1)S(1)} %get-tuple-element.642, bf16[8,1024,128]{1,2,0:T(8,128)(2,1)} %get-tuple-element.641, s32[]{:T(128)S(6)} %copy.45), kind=kOutput, calls=%fused_computation.12.clone.1 | convolution fusion | flops 543161344 | bytes 11276292 | tf_op jit(solution)/shard_map/while/body/eval_jaxpr/while/body/eval_jaxpr/dot_general | solution.py:71
  164.2 3.0 %fusion.135 = f32[1024]{0:T(1024)S(1)} fusion(pred[1024,2048]{1,0:T(32,128)(4,1)S(1)} %copy-done.1, f32[1024,2048]{1,0:T(8,128)S(1)} %get-tuple-element.610, f32[1024]{0:T(1024)S(1)} %get-tuple-element.611), kind=kLoop, calls=%fused_computation.13.clone.1 | loop fusion | flops 10484736 | bytes 10493952 | tf_op jit(solution)/shard_map/while/body/eval_jaxpr/while/body/eval_jaxpr/reduce_sum | solution.py:78
  167.9 3.5 %fusion.136 = bf16[8,1024,128]{2,1,0:T(8,128)(2,1)} fusion(bf16[8,1024,128]{2,1,0:T(8,128)(2,1)} %get-tuple-element.631, s32[]{:T(128)S(6)} %copy.45, bf16[2048,128]{1,0:T(8,128)(2,1)S(1)} %get-tuple-element.644, pred[1024,2048]{1,0:T(32,128)(4,1)S(1)} %copy-done.1, f32[1024,2048]{1,0:T(8,128)S(1)} %get-tuple-element.610, ...), kind=kOutput, calls=%fused_computation.20.clone.1 | convolution fusion | flops 547749888 | bytes 11281412 | tf_op jit(solution)/shard_map/while/body/eval_jaxpr/while/body/eval_jaxpr/dot_general | solution.py:79
  171.4 3.8 %fusion.134 = (f32[1024]{0:T(1024)S(1)}, f32[1024,2048]{1,0:T(8,128)S(1)}) fusion(pred[1024,2048]{1,0:T(32,128)(4,1)} %get-tuple-element.643, bf16[2048,128]{1,0:T(8,128)(2,1)S(1)} %get-tuple-element.642, bf16[8,1024,128]{1,2,0:T(8,128)(2,1)} %get-tuple-element.641, s32[]{:T(128)S(6)} %copy.45), kind=kOutput, calls=%fused_computation.12.clone.1 | convolution fusion | flops 543161344 | bytes 11276292 | tf_op jit(solution)/shard_map/while/body/eval_jaxpr/while/body/eval_jaxpr/dot_general | solution.py:71
  175.2 3.0 %fusion.135 = f32[1024]{0:T(1024)S(1)} fusion(pred[1024,2048]{1,0:T(32,128)(4,1)S(1)} %copy-done.1, f32[1024,2048]{1,0:T(8,128)S(1)} %get-tuple-element.610, f32[1024]{0:T(1024)S(1)} %get-tuple-element.611), kind=kLoop, calls=%fused_computation.13.clone.1 | loop fusion | flops 10484736 | bytes 10493952 | tf_op jit(solution)/shard_map/while/body/eval_jaxpr/while/body/eval_jaxpr/reduce_sum | solution.py:78
  178.9 3.5 %fusion.136 = bf16[8,1024,128]{2,1,0:T(8,128)(2,1)} fusion(bf16[8,1024,128]{2,1,0:T(8,128)(2,1)} %get-tuple-element.631, s32[]{:T(128)S(6)} %copy.45, bf16[2048,128]{1,0:T(8,128)(2,1)S(1)} %get-tuple-element.644, pred[1024,2048]{1,0:T(32,128)(4,1)S(1)} %copy-done.1, f32[1024,2048]{1,0:T(8,128)S(1)} %get-tuple-element.610, ...), kind=kOutput, calls=%fused_computation.20.clone.1 | convolution fusion | flops 547749888 | bytes 11281412 | tf_op jit(solution)/shard_map/while/body/eval_jaxpr/while/body/eval_jaxpr/dot_general | solution.py:79
  182.4 3.8 %fusion.134 = (f32[1024]{0:T(1024)S(1)}, f32[1024,2048]{1,0:T(8,128)S(1)}) fusion(pred[1024,2048]{1,0:T(32,128)(4,1)} %get-tuple-element.643, bf16[2048,128]{1,0:T(8,128)(2,1)S(1)} %get-tuple-element.642, bf16[8,1024,128]{1,2,0:T(8,128)(2,1)} %get-tuple-element.641, s32[]{:T(128)S(6)} %copy.45), kind=kOutput, calls=%fused_computation.12.clone.1 | convolution fusion | flops 543161344 | bytes 11276292 | tf_op jit(solution)/shard_map/while/body/eval_jaxpr/while/body/eval_jaxpr/dot_general | solution.py:71
  186.3 3.0 %fusion.135 = f32[1024]{0:T(1024)S(1)} fusion(pred[1024,2048]{1,0:T(32,128)(4,1)S(1)} %copy-done.1, f32[1024,2048]{1,0:T(8,128)S(1)} %get-tuple-element.610, f32[1024]{0:T(1024)S(1)} %get-tuple-element.611), kind=kLoop, calls=%fused_computation.13.clone.1 | loop fusion | flops 10484736 | bytes 10493952 | tf_op jit(solution)/shard_map/while/body/eval_jaxpr/while/body/eval_jaxpr/reduce_sum | solution.py:78
  190.0 3.5 %fusion.136 = bf16[8,1024,128]{2,1,0:T(8,128)(2,1)} fusion(bf16[8,1024,128]{2,1,0:T(8,128)(2,1)} %get-tuple-element.631, s32[]{:T(128)S(6)} %copy.45, bf16[2048,128]{1,0:T(8,128)(2,1)S(1)} %get-tuple-element.644, pred[1024,2048]{1,0:T(32,128)(4,1)S(1)} %copy-done.1, f32[1024,2048]{1,0:T(8,128)S(1)} %get-tuple-element.610, ...), kind=kOutput, calls=%fused_computation.20.clone.1 | convolution fusion | flops 547749888 | bytes 11281412 | tf_op jit(solution)/shard_map/while/body/eval_jaxpr/while/body/eval_jaxpr/dot_general | solution.py:79
  193.5 3.8 %fusion.134 = (f32[1024]{0:T(1024)S(1)}, f32[1024,2048]{1,0:T(8,128)S(1)}) fusion(pred[1024,2048]{1,0:T(32,128)(4,1)} %get-tuple-element.643, bf16[2048,128]{1,0:T(8,128)(2,1)S(1)} %get-tuple-element.642, bf16[8,1024,128]{1,2,0:T(8,128)(2,1)} %get-tuple-element.641, s32[]{:T(128)S(6)} %copy.45), kind=kOutput, calls=%fused_computation.12.clone.1 | convolution fusion | flops 543161344 | bytes 11276292 | tf_op jit(solution)/shard_map/while/body/eval_jaxpr/while/body/eval_jaxpr/dot_general | solution.py:71
  197.3 3.0 %fusion.135 = f32[1024]{0:T(1024)S(1)} fusion(pred[1024,2048]{1,0:T(32,128)(4,1)S(1)} %copy-done.1, f32[1024,2048]{1,0:T(8,128)S(1)} %get-tuple-element.610, f32[1024]{0:T(1024)S(1)} %get-tuple-element.611), kind=kLoop, calls=%fused_computation.13.clone.1 | loop fusion | flops 10484736 | bytes 10493952 | tf_op jit(solution)/shard_map/while/body/eval_jaxpr/while/body/eval_jaxpr/reduce_sum | solution.py:78
  201.0 3.5 %fusion.136 = bf16[8,1024,128]{2,1,0:T(8,128)(2,1)} fusion(bf16[8,1024,128]{2,1,0:T(8,128)(2,1)} %get-tuple-element.631, s32[]{:T(128)S(6)} %copy.45, bf16[2048,128]{1,0:T(8,128)(2,1)S(1)} %get-tuple-element.644, pred[1024,2048]{1,0:T(32,128)(4,1)S(1)} %copy-done.1, f32[1024,2048]{1,0:T(8,128)S(1)} %get-tuple-element.610, ...), kind=kOutput, calls=%fused_computation.20.clone.1 | convolution fusion | flops 547749888 | bytes 11281412 | tf_op jit(solution)/shard_map/while/body/eval_jaxpr/while/body/eval_jaxpr/dot_general | solution.py:79
  204.5 3.8 %fusion.134 = (f32[1024]{0:T(1024)S(1)}, f32[1024,2048]{1,0:T(8,128)S(1)}) fusion(pred[1024,2048]{1,0:T(32,128)(4,1)} %get-tuple-element.643, bf16[2048,128]{1,0:T(8,128)(2,1)S(1)} %get-tuple-element.642, bf16[8,1024,128]{1,2,0:T(8,128)(2,1)} %get-tuple-element.641, s32[]{:T(128)S(6)} %copy.45), kind=kOutput, calls=%fused_computation.12.clone.1 | convolution fusion | flops 543161344 | bytes 11276292 | tf_op jit(solution)/shard_map/while/body/eval_jaxpr/while/body/eval_jaxpr/dot_general | solution.py:71
  208.4 3.0 %fusion.135 = f32[1024]{0:T(1024)S(1)} fusion(pred[1024,2048]{1,0:T(32,128)(4,1)S(1)} %copy-done.1, f32[1024,2048]{1,0:T(8,128)S(1)} %get-tuple-element.610, f32[1024]{0:T(1024)S(1)} %get-tuple-element.611), kind=kLoop, calls=%fused_computation.13.clone.1 | loop fusion | flops 10484736 | bytes 10493952 | tf_op jit(solution)/shard_map/while/body/eval_jaxpr/while/body/eval_jaxpr/reduce_sum | solution.py:78
  212.1 3.5 %fusion.136 = bf16[8,1024,128]{2,1,0:T(8,128)(2,1)} fusion(bf16[8,1024,128]{2,1,0:T(8,128)(2,1)} %get-tuple-element.631, s32[]{:T(128)S(6)} %copy.45, bf16[2048,128]{1,0:T(8,128)(2,1)S(1)} %get-tuple-element.644, pred[1024,2048]{1,0:T(32,128)(4,1)S(1)} %copy-done.1, f32[1024,2048]{1,0:T(8,128)S(1)} %get-tuple-element.610, ...), kind=kOutput, calls=%fused_computation.20.clone.1 | convolution fusion | flops 547749888 | bytes 11281412 | tf_op jit(solution)/shard_map/while/body/eval_jaxpr/while/body/eval_jaxpr/dot_general | solution.py:79
  215.6 3.8 %fusion.134 = (f32[1024]{0:T(1024)S(1)}, f32[1024,2048]{1,0:T(8,128)S(1)}) fusion(pred[1024,2048]{1,0:T(32,128)(4,1)} %get-tuple-element.643, bf16[2048,128]{1,0:T(8,128)(2,1)S(1)} %get-tuple-element.642, bf16[8,1024,128]{1,2,0:T(8,128)(2,1)} %get-tuple-element.641, s32[]{:T(128)S(6)} %copy.45), kind=kOutput, calls=%fused_computation.12.clone.1 | convolution fusion | flops 543161344 | bytes 11276292 | tf_op jit(solution)/shard_map/while/body/eval_jaxpr/while/body/eval_jaxpr/dot_general | solution.py:71
  219.4 3.0 %fusion.135 = f32[1024]{0:T(1024)S(1)} fusion(pred[1024,2048]{1,0:T(32,128)(4,1)S(1)} %copy-done.1, f32[1024,2048]{1,0:T(8,128)S(1)} %get-tuple-element.610, f32[1024]{0:T(1024)S(1)} %get-tuple-element.611), kind=kLoop, calls=%fused_computation.13.clone.1 | loop fusion | flops 10484736 | bytes 10493952 | tf_op jit(solution)/shard_map/while/body/eval_jaxpr/while/body/eval_jaxpr/reduce_sum | solution.py:78
  223.1 3.5 %fusion.136 = bf16[8,1024,128]{2,1,0:T(8,128)(2,1)} fusion(bf16[8,1024,128]{2,1,0:T(8,128)(2,1)} %get-tuple-element.631, s32[]{:T(128)S(6)} %copy.45, bf16[2048,128]{1,0:T(8,128)(2,1)S(1)} %get-tuple-element.644, pred[1024,2048]{1,0:T(32,128)(4,1)S(1)} %copy-done.1, f32[1024,2048]{1,0:T(8,128)S(1)} %get-tuple-element.610, ...), kind=kOutput, calls=%fused_computation.20.clone.1 | convolution fusion | flops 547749888 | bytes 11281412 | tf_op jit(solution)/shard_map/while/body/eval_jaxpr/while/body/eval_jaxpr/dot_general | solution.py:79
  226.6 3.8 %fusion.134 = (f32[1024]{0:T(1024)S(1)}, f32[1024,2048]{1,0:T(8,128)S(1)}) fusion(pred[1024,2048]{1,0:T(32,128)(4,1)} %get-tuple-element.643, bf16[2048,128]{1,0:T(8,128)(2,1)S(1)} %get-tuple-element.642, bf16[8,1024,128]{1,2,0:T(8,128)(2,1)} %get-tuple-element.641, s32[]{:T(128)S(6)} %copy.45), kind=kOutput, calls=%fused_computation.12.clone.1 | convolution fusion | flops 543161344 | bytes 11276292 | tf_op jit(solution)/shard_map/while/body/eval_jaxpr/while/body/eval_jaxpr/dot_general | solution.py:71
  230.5 3.0 %fusion.135 = f32[1024]{0:T(1024)S(1)} fusion(pred[1024,2048]{1,0:T(32,128)(4,1)S(1)} %copy-done.1, f32[1024,2048]{1,0:T(8,128)S(1)} %get-tuple-element.610, f32[1024]{0:T(1024)S(1)} %get-tuple-element.611), kind=kLoop, calls=%fused_computation.13.clone.1 | loop fusion | flops 10484736 | bytes 10493952 | tf_op jit(solution)/shard_map/while/body/eval_jaxpr/while/body/eval_jaxpr/reduce_sum | solution.py:78
  234.2 3.5 %fusion.136 = bf16[8,1024,128]{2,1,0:T(8,128)(2,1)} fusion(bf16[8,1024,128]{2,1,0:T(8,128)(2,1)} %get-tuple-element.631, s32[]{:T(128)S(6)} %copy.45, bf16[2048,128]{1,0:T(8,128)(2,1)S(1)} %get-tuple-element.644, pred[1024,2048]{1,0:T(32,128)(4,1)S(1)} %copy-done.1, f32[1024,2048]{1,0:T(8,128)S(1)} %get-tuple-element.610, ...), kind=kOutput, calls=%fused_computation.20.clone.1 | convolution fusion | flops 547749888 | bytes 11281412 | tf_op jit(solution)/shard_map/while/body/eval_jaxpr/while/body/eval_jaxpr/dot_general | solution.py:79
  237.7 2.9 %copy.23 = bf16[1024,1,8,128]{3,2,0,1:T(8,128)(2,1)S(1)} copy(bf16[1024,1,8,128]{3,0,2,1:T(8,128)(2,1)} %bitcast.111) | data formatting | bytes 4194304 | tf_op jit(solution)/shard_map/transpose | solution.py:161
  240.6 1.9 copy.37
  242.6 1.5 convert_element_type.62
  (124 shorter events, 28.3 us)
Async XLA Ops:
  7.2 140.9 %copy-start = (bf16[1024,1024]{1,0:T(8,128)(2,1)S(1)}, bf16[1024,1024]{1,0:T(8,128)(2,1)}, u32[]{:S(2)}) copy-start(bf16[1024,1024]{1,0:T(8,128)(2,1)} %param.17) | copy-start | bytes 6291460
  7.2 5.6 %copy-start.3 = (bf16[1024,128]{1,0:T(8,128)(2,1)S(1)}, bf16[1024,128]{1,0:T(8,128)(2,1)}, u32[]{:S(2)}) copy-start(bf16[1024,128]{1,0:T(8,128)(2,1)} %param.15) | copy-start | bytes 786436
  7.2 5.9 %copy-start.5 = (bf16[8,1024]{1,0:T(8,128)(2,1)S(1)}, bf16[8,1024]{1,0:T(8,128)(2,1)}, u32[]{:S(2)}) copy-start(bf16[8,1024]{1,0:T(8,128)(2,1)} %param.16) | copy-start | bytes 49156
  7.2 127.1 %all-reduce.2.cloned.1.call-start = ((), (), s32[]{:S(2)}) async-start(), calls=%async_computation.1 | async-start | bytes 1048576 | tf_op jit(solution)/shard_map/psum | solution.py:18
  11.4 126.5 %all-gather.5.cloned.1.call-start = ((), (), s32[]{:S(2)}) async-start(), calls=%async_computation.3 | async-start | bytes 2359296 | tf_op jit(solution)/shard_map/all_gather | solution.py:22
  13.1 33.5 %copy-start.6 = (s32[8]{0:T(128)S(1)}, s32[8]{0:T(128)}, u32[]{:S(2)}) copy-start(s32[8]{0:T(128)} %param.19) | copy-start | bytes 100
  65.0 177.6 %reduce-scatter.2.cloned.1.call-start = ((), (), s32[]{:S(2)}) async-start(), calls=%async_computation.2 | async-start | bytes 327680 | tf_op jit(solution)/shard_map/reduce_scatter | solution.py:181
  131.9 3.5 %copy-start.2 = (bf16[1024,128]{1,0:T(8,128)(2,1)S(1)}, bf16[1024,128]{1,0:T(8,128)(2,1)}, u32[]{:S(2)}) copy-start(bf16[1024,128]{1,0:T(8,128)(2,1)} %param.14) | copy-start | bytes 786436
  147.7 1.6 copy-start.4
  149.3 3.8 %copy-start.1 = (pred[1024,2048]{1,0:T(32,128)(4,1)S(1)}, pred[1024,2048]{1,0:T(32,128)(4,1)}, u32[]{:S(2)}) copy-start(pred[1024,2048]{1,0:T(32,128)(4,1)} %get-tuple-element.643) | copy-start | bytes 6291460 | tf_op jit(solution)/shard_map/while/body/eval_jaxpr/while
  160.3 3.8 %copy-start.1 = (pred[1024,2048]{1,0:T(32,128)(4,1)S(1)}, pred[1024,2048]{1,0:T(32,128)(4,1)}, u32[]{:S(2)}) copy-start(pred[1024,2048]{1,0:T(32,128)(4,1)} %get-tuple-element.643) | copy-start | bytes 6291460 | tf_op jit(solution)/shard_map/while/body/eval_jaxpr/while
  171.4 3.8 %copy-start.1 = (pred[1024,2048]{1,0:T(32,128)(4,1)S(1)}, pred[1024,2048]{1,0:T(32,128)(4,1)}, u32[]{:S(2)}) copy-start(pred[1024,2048]{1,0:T(32,128)(4,1)} %get-tuple-element.643) | copy-start | bytes 6291460 | tf_op jit(solution)/shard_map/while/body/eval_jaxpr/while
  182.4 3.8 %copy-start.1 = (pred[1024,2048]{1,0:T(32,128)(4,1)S(1)}, pred[1024,2048]{1,0:T(32,128)(4,1)}, u32[]{:S(2)}) copy-start(pred[1024,2048]{1,0:T(32,128)(4,1)} %get-tuple-element.643) | copy-start | bytes 6291460 | tf_op jit(solution)/shard_map/while/body/eval_jaxpr/while
  193.5 3.8 %copy-start.1 = (pred[1024,2048]{1,0:T(32,128)(4,1)S(1)}, pred[1024,2048]{1,0:T(32,128)(4,1)}, u32[]{:S(2)}) copy-start(pred[1024,2048]{1,0:T(32,128)(4,1)} %get-tuple-element.643) | copy-start | bytes 6291460 | tf_op jit(solution)/shard_map/while/body/eval_jaxpr/while
  204.5 3.8 %copy-start.1 = (pred[1024,2048]{1,0:T(32,128)(4,1)S(1)}, pred[1024,2048]{1,0:T(32,128)(4,1)}, u32[]{:S(2)}) copy-start(pred[1024,2048]{1,0:T(32,128)(4,1)} %get-tuple-element.643) | copy-start | bytes 6291460 | tf_op jit(solution)/shard_map/while/body/eval_jaxpr/while
  215.6 3.8 %copy-start.1 = (pred[1024,2048]{1,0:T(32,128)(4,1)S(1)}, pred[1024,2048]{1,0:T(32,128)(4,1)}, u32[]{:S(2)}) copy-start(pred[1024,2048]{1,0:T(32,128)(4,1)} %get-tuple-element.643) | copy-start | bytes 6291460 | tf_op jit(solution)/shard_map/while/body/eval_jaxpr/while
  226.6 3.8 %copy-start.1 = (pred[1024,2048]{1,0:T(32,128)(4,1)S(1)}, pred[1024,2048]{1,0:T(32,128)(4,1)}, u32[]{:S(2)}) copy-start(pred[1024,2048]{1,0:T(32,128)(4,1)} %get-tuple-element.643) | copy-start | bytes 6291460 | tf_op jit(solution)/shard_map/while/body/eval_jaxpr/while
Sparse Core Ops, SparseCore 0:
  11.5 75.2 all-reduce.1
  89.1 48.7 all-gather.4
  149.4 19.5 reduce-scatter.1
where the time goes:
time: 251 us
  blocking collectives  93.6 us (37%)
  matrix products  71.4 us (28%)
  other arithmetic  55.9 us (22%)
  between operations  15.4 us (6%)
  local copies, waits for them, and re-layouts  12 us (5%)
    all_gather x2, blocking collectives, joined(): gathered = jax.tree.map(lambda a: lax.all_gather(a, axis), part)  61.2 us
    all_gather x1, blocking collectives, per_device(): gathered = lax.all_gather(new_queries, 'ctx', axis=0, tiled=True)  32.5 us
    dot_general x8, matrix products, block_single_head(): jnp.dot(query_rows, all_keys.T, preferred_element_type=jnp.float32)  30.6 us
    dot_general x8, matrix products, block_single_head(): jnp.dot(weights, all_values, preferred_element_type=jnp.float32)  28.2 us
    reduce_sum x8, other arithmetic, block_single_head(): totals = jnp.sum(powers, axis=1)  24 us
    add x7, other arithmetic, merge_pair(): first[2] * first_factor[..., None] + second[2] * second_factor[..., None]  8.49 us
    dot_general x8, matrix products, host_single_head(): jnp.dot(weights, rot_values, preferred_element_type=jnp.float32)  6.79 us
    unnamed x17, local copies, waits for them, and re-layouts  6.3 us
  transfers between devices with their start and end apart: 3, of which 1 were waited for; matrix products, arithmetic and copies ran while one was open for 49% of the time, Pallas kernels for 0%

commit v1 on v0

v1 whole, which is shorter than its diff:
```python
import functools

import jax
import jax.numpy as jnp
from jax import lax
from jax.experimental import pallas as pl
from jax.experimental.pallas import tpu as pltpu
from jax.sharding import PartitionSpec as P

HD = 128
CLIP_FACTOR = 2.0
NEG = -1e30
LOG2E = 1.4426950408889634
NT = (((1,), (1,)), ((), ()))
SPREAD = 4
SPREAD_BITS = (1, 2)
TAIL = 8
F32 = jnp.float32
BF16 = jnp.bfloat16


def sign_table(size):
    a = lax.broadcasted_iota(jnp.int32, (size, size), 0)
    b = lax.broadcasted_iota(jnp.int32, (size, size), 1)
    x = jnp.bitwise_and(a, b)
    parity = jnp.zeros((size, size), jnp.int32)
    for bit in range(int(size).bit_length()):
        parity = jnp.bitwise_xor(parity, jnp.bitwise_and(jnp.right_shift(x, bit), 1))
    return (1 - 2 * parity).astype(F32)


def context_kernel(lens, q_ref, k_ref, v_ref, ak_ref, av_ref, o_ref, *, tq, tk, hp, st):
    own_len, anchor_len, anchor_tiles = lens[0], lens[1], lens[2]
    rows, hd = k_ref.shape
    c = hd**-0.5 * LOG2E

    def scores(na, h, i):
        q = [q_ref[i * tq : (i + 1) * tq, (h + e) * hd : (h + e + 1) * hd] for e in range(st)]
        q = jnp.concatenate(q, axis=0)
        parts = []
        if na:
            edge = (na - 1) * tk
            sa = lax.dot_general(q, ak_ref[: na * tk], NT, preferred_element_type=F32)
            col = lax.broadcasted_iota(jnp.int32, (1, tk), 1)
            if na > 1:
                parts.append((sa[:, :edge], av_ref, 0))
            parts.append((jnp.where(col < anchor_len - edge, sa[:, edge:], NEG), av_ref, edge))
        so = lax.dot_general(q, k_ref[: (i + 1) * tq], NT, preferred_element_type=F32)
        r0 = lax.broadcasted_iota(jnp.int32, (tq, tq), 0)
        c0 = lax.broadcasted_iota(jnp.int32, (tq, tq), 1)
        seen = c0 <= r0
        d = [jnp.where(seen, so[e * tq : (e + 1) * tq, i * tq :], NEG) for e in range(st)]
        if i:
            parts.append((so[:, : i * tq], v_ref, 0))
        parts.append((jnp.concatenate(d, axis=0), v_ref, i * tq))
        return parts

    def fold(op, xs):
        return functools.reduce(
            op, [x[:, a : a + 128] for x in xs for a in range(0, x.shape[1], 128)]
        )

    def finish(parts, h, i):
        m = jnp.max(fold(jnp.maximum, [p for p, _, _ in parts]), axis=1, keepdims=True)
        acc = 0.0
        powers = []
        for p, src, at in parts:
            e = jnp.exp2((p - m) * c)
            powers.append(e)
            acc = acc + jnp.dot(
                e.astype(BF16), src[at : at + p.shape[1]], preferred_element_type=F32
            )
        total = jnp.sum(fold(jnp.add, powers), axis=1, keepdims=True)
        row = lax.broadcasted_iota(jnp.int32, (tq, 1), 0) + i * tq
        for e in range(st):
            part = slice(e * tq, (e + 1) * tq)
            out = jnp.where(row < own_len, acc[part] / total[part], 0.0)
            o_ref[i * tq : (i + 1) * tq, (h + e) * hd : (h + e + 1) * hd] = out.astype(BF16)

    def body(na):
        pending = None
        for h in range(0, hp, st):
            for i in range(rows // tq):
                s = scores(na, h, i)
                if pending is not None:
                    finish(*pending)
                pending = (s, h, i)
        finish(*pending)

    for na in range(rows // tk + 1):
        pl.when(anchor_tiles == na)(functools.partial(body, na))


def context_attention(lens, q, k, v, ak, av, tq=128, tk=256, hp=4, st=4):
    rows, width = q.shape
    hd = k.shape[1]
    heads = width // hd
    full = pl.BlockSpec((rows, hd), lambda h, *_: (0, 0))
    wide = pl.BlockSpec((rows, hp * hd), lambda h, *_: (0, h))
    return pl.pallas_call(
        functools.partial(context_kernel, tq=tq, tk=tk, hp=hp, st=st),
        grid_spec=pltpu.PrefetchScalarGridSpec(
            num_scalar_prefetch=1,
            grid=(heads // hp,),
            in_specs=[wide, full, full, full, full],
            out_specs=wide,
        ),
        out_shape=jax.ShapeDtypeStruct(q.shape, q.dtype),
        compiler_params=pltpu.CompilerParams(vmem_limit_bytes=40 << 20),
        cost_estimate=pl.CostEstimate(
            flops=24 * heads * rows * rows * hd // 4,
            bytes_accessed=4 * rows * width + 8 * rows * hd,
            transcendentals=heads * rows * rows * 3 // 2,
        ),
        name="context_attention",
    )(lens, q, k, v, ak, av)


def partial_kernel(scal, *refs, hd, step, blocks):
    q_refs, (k_ref, v_ref), outs, (q_all,) = (
        refs[:SPREAD],
        refs[SPREAD : SPREAD + 2],
        refs[SPREAD + 2 : -1],
        refs[-1:],
    )
    spot, own_len = scal[0], scal[1]
    tokens, width = q_all.shape
    per = width // hd // SPREAD
    scale = hd**-0.5
    table = sign_table(hd)
    table16 = table.astype(BF16)
    for k in range(SPREAD):
        for x in range(blocks):
            at = pl.multiple_of((x * SPREAD + jnp.bitwise_xor(spot, k)) * step, step)
            q_all[pl.ds(at, step), :] = q_refs[k][x * step : (x + 1) * step, :]

    def store(ref):
        r = jnp.dot(ref[...], table16, preferred_element_type=F32) * scale
        ceiling = CLIP_FACTOR * jnp.sqrt(jnp.mean(r * r, axis=-1, keepdims=True))
        return jnp.clip(r, -ceiling, ceiling)

    key_store = store(k_ref).astype(BF16)
    value_turned = store(v_ref).T.astype(BF16)
    rows = k_ref.shape[0]
    usable = lax.broadcasted_iota(jnp.int32, (rows, 1), 0) < own_len
    for k in range(SPREAD):
        at = pl.multiple_of(jnp.bitwise_xor(spot, k) * (per * hd), per * hd)
        q = q_all[:, pl.ds(at, per * hd)]
        q = jnp.concatenate([q[:, e * hd : (e + 1) * hd] for e in range(per)], axis=0)
        rot = (jnp.dot(q, table16, preferred_element_type=F32) * scale).astype(BF16)
        s = lax.dot_general(key_store, rot, NT, preferred_element_type=F32) * scale
        s = jnp.where(usable, s, NEG)
        m = jnp.max(s, axis=0, keepdims=True)
        p = jnp.exp(s - m)
        total = jnp.sum(p, axis=0, keepdims=True)
        outs[k][:hd, :] = jnp.dot(value_turned, p.astype(BF16), preferred_element_type=F32)
        outs[k][hd : hd + 1, :] = m
        outs[k][hd + 1 : hd + 2, :] = total
        outs[k][hd + 2 :, :] = jnp.zeros((TAIL - 2, q.shape[0]), F32)


def host_partials(spot, own_len, pieces, keys, values, heads):
    hd = keys.shape[1]
    width = pieces[0].shape[1]
    tokens = SPREAD * pieces[0].shape[0]
    blocks = pieces[0].shape[0] // 16
    shape = jax.ShapeDtypeStruct((hd + TAIL, tokens * heads // SPREAD), F32)
    whole = pl.BlockSpec(memory_space=pltpu.VMEM)
    return pl.pallas_call(
        functools.partial(partial_kernel, hd=hd, step=16, blocks=blocks),
        in_specs=[pl.BlockSpec(memory_space=pltpu.SMEM)] + [whole] * (SPREAD + 2),
        out_specs=[whole] * SPREAD,
        out_shape=[shape] * SPREAD,
        scratch_shapes=[pltpu.VMEM((tokens, width), BF16)],
        compiler_params=pltpu.CompilerParams(vmem_limit_bytes=24 << 20),
        name="host_partials",
    )(jnp.stack([spot, own_len]), *pieces, keys, values)


def merge_values(parts, hd):
    maxima = [p[hd : hd + 1, :] for p in parts]
    overall = functools.reduce(jnp.maximum, maxima)
    factors = [jnp.exp(m - overall) for m in maxima]
    out = sum(p[:hd, :] * f for p, f in zip(parts, factors))
    total = sum(p[hd + 1 : hd + 2, :] * f for p, f in zip(parts, factors))
    return overall, total, out


def merge_kernel(*refs, hd):
    o_ref = refs[-1]
    overall, total, out = merge_values(refs[:-1], hd)
    o_ref[:hd, :] = out
    o_ref[hd : hd + 1, :] = overall
    o_ref[hd + 1 : hd + 2, :] = total
    o_ref[hd + 2 :, :] = jnp.zeros((TAIL - 2, out.shape[1]), F32)


def merged(parts, hd):
    whole = pl.BlockSpec(memory_space=pltpu.VMEM)
    return pl.pallas_call(
        functools.partial(merge_kernel, hd=hd),
        in_specs=[whole] * len(parts),
        out_specs=whole,
        out_shape=jax.ShapeDtypeStruct(parts[0].shape, F32),
        name="merge_partials",
    )(*parts)


def finish_kernel(*refs, hd, tokens):
    o_ref = refs[-1]
    _, total, out = merge_values(refs[:-1], hd)
    turned = jnp.dot(
        sign_table(hd),
        out / total,
        preferred_element_type=F32,
        precision=lax.Precision.HIGHEST,
    )
    turned = (turned * hd**-0.5).T
    for e in range(turned.shape[0] // tokens):
        o_ref[:, e * hd : (e + 1) * hd] = turned[e * tokens : (e + 1) * tokens].astype(BF16)


def finished(parts, hd, tokens):
    whole = pl.BlockSpec(memory_space=pltpu.VMEM)
    per = parts[0].shape[1] // tokens
    return pl.pallas_call(
        functools.partial(finish_kernel, hd=hd, tokens=tokens),
        in_specs=[whole] * len(parts),
        out_specs=whole,
        out_shape=jax.ShapeDtypeStruct((tokens, per * hd), BF16),
        name="finish_queries",
    )(*parts)


def project_kernel(scal, *refs, groups):
    a_refs, w_ref, outs, total = refs[:SPREAD], refs[SPREAD], refs[SPREAD + 1 : -1], refs[-1]
    spot, head = scal[0], scal[1]
    depth = a_refs[0].shape[1]
    acc = 0.0
    for k in range(SPREAD):
        at = pl.multiple_of(jnp.bitwise_xor(spot, k) * depth, depth)
        acc = acc + jnp.dot(a_refs[k][...], w_ref[pl.ds(at, depth), :], preferred_element_type=F32)
    total[...] = acc
    rows = total.shape[0] // groups
    for k in range(groups):
        at = pl.multiple_of(jnp.bitwise_xor(head, k) * rows, rows)
        outs[k][...] = total[pl.ds(at, rows), :]


def projected(spot, head, chunks, weight, groups):
    tokens = chunks[0].shape[0]
    columns = weight.shape[1]
    whole = pl.BlockSpec(memory_space=pltpu.VMEM)
    return pl.pallas_call(
        functools.partial(project_kernel, groups=groups),
        in_specs=[pl.BlockSpec(memory_space=pltpu.SMEM)] + [whole] * (SPREAD + 1),
        out_specs=[whole] * groups,
        out_shape=[jax.ShapeDtypeStruct((tokens // groups, columns), F32)] * groups,
        scratch_shapes=[pltpu.VMEM((tokens, columns), F32)],
        compiler_params=pltpu.CompilerParams(vmem_limit_bytes=16 << 20),
        name="project",
    )(jnp.stack([spot, head]), *chunks, weight)


def swap(x, axis, flip):
    size = lax.axis_size(axis)
    return lax.ppermute(x, axis, [(i, i ^ flip) for i in range(size)])


def per_device(
    ctx_queries, ctx_keys, ctx_values, new_queries, out_weight, host_block, block_lengths
):
    hosts = lax.axis_size("ctx")
    groups = lax.axis_size("head")
    bits = hosts.bit_length() - 1
    other_bits = [b for b in range(bits) if b not in SPREAD_BITS]
    heads = ctx_queries.shape[1] // HD
    tokens = new_queries.shape[0] * hosts
    me = lax.axis_index("ctx").astype(jnp.int32)
    head = lax.axis_index("head").astype(jnp.int32)
    spot = jnp.bitwise_and(jnp.right_shift(me, 1), SPREAD - 1)

    host_ids = jnp.arange(hosts, dtype=jnp.int32)
    own_block = jnp.sum(jnp.where(host_ids == me, host_block, 0))
    own_len = jnp.sum(jnp.where(host_ids == own_block, block_lengths, 0))
    root = jnp.sum(jnp.where(host_block == 0, host_ids, 0))
    anchor_len = block_lengths[0]
    is_anchor = own_block == 0

    def bit(value, b):
        return jnp.bitwise_and(jnp.right_shift(value, b), 1)

    piece = new_queries
    for b in other_bits:
        got = swap(piece, "ctx", 1 << b)
        low = bit(me, b) == 0
        piece = jnp.concatenate([jnp.where(low, piece, got), jnp.where(low, got, piece)], axis=0)
    pieces = [piece] + [swap(piece, "ctx", k << 1) for k in range(1, SPREAD)]

    even = bit(me, 0) == 0
    held = jnp.where(even, ctx_keys, ctx_values)
    got = swap(jnp.where(even, ctx_values, ctx_keys), "ctx", 1)
    held = jnp.where(bit(root, 0) == bit(me, 0), held, got)
    for b in range(1, bits):
        got = swap(held, "ctx", 1 << b)
        held = jnp.where(bit(root, b) == bit(me, b), held, got)
    got = swap(held, "ctx", 1)
    anchor_k = jnp.where(even, held, got)
    anchor_v = jnp.where(even, got, held)

    partials = host_partials(spot, own_len, pieces, ctx_keys, ctx_values, heads)
    parts = [partials[0]] + [swap(partials[k], "ctx", k << 1) for k in range(1, SPREAD)]
    one = merged(parts, HD)
    for b in other_bits[1:]:
        one = merged([one, swap(one, "ctx", 1 << b)], HD)
    chunk = finished([one, swap(one, "ctx", 1)], HD, tokens)
    chunks = [chunk] + [swap(chunk, "ctx", k << 1) for k in range(1, SPREAD)]
    sums = projected(spot, head, chunks, out_weight, groups)
    answer = sums[0]
    for k in range(1, groups):
        answer = answer + swap(sums[k], "head", k)
    answer = answer.astype(BF16)

    tile = 256
    anchor_tiles = jnp.where(is_anchor, 0, (anchor_len + tile - 1) // tile)
    lens = jnp.stack([own_len, anchor_len, anchor_tiles]).astype(jnp.int32)
    context_out = context_attention(
        lens, ctx_queries, ctx_keys, ctx_values, anchor_k, anchor_v, tk=tile
    )
    return (context_out, answer)


def solution(mesh):
    placed = (
        P("ctx", "head"),
        P("ctx", "head"),
        P("ctx", "head"),
        P("ctx", "head"),
        P("head", "ctx"),
        P(),
        P(),
    )
    return jax.shard_map(
        per_device,
        mesh=mesh,
        in_specs=placed,
        out_specs=(P("ctx", "head"), P("head", "ctx")),
        check_vma=False,
    )
```

time: 251 us -> 110 us (0.44)
  blocking collectives: 93.6 us -> 0 us
  matrix products: 71.4 us -> 0 us
  other arithmetic: 55.9 us -> 8.37 us
  Pallas kernels: 0 us -> 45.5 us
  starting transfers between devices: 0.12 us -> 26.9 us
  waiting for transfers between devices: 1.65 us -> 20.5 us
  between operations: 15.4 us -> 3.81 us
  local copies, waits for them, and re-layouts: 12 us -> 2.69 us
    all_gather x3 -> x0, blocking collectives: 93.6 us -> none  [the longest x2 61.2 us: joined(): gathered = jax.tree.map(lambda a: lax.all_gather(a, axis), part)]
    dot_general x37 -> x0, matrix products: 71.4 us -> none  [the longest x8 30.6 us: block_single_head(): jnp.dot(query_rows, all_keys.T, preferred_element_type=jnp.float32)]
    pallas_call x0 -> x5, Pallas kernels: none -> 45.5 us  [the longest x1 37.7 us: context_attention(): pl.pallas_call(functools.partial(context_kernel, tq=tq, tk=tk, hp=hp, st=...]
    ppermute x0 -> x18, starting transfers between devices: none -> 26.9 us  [swap(): return lax.ppermute(x, axis, [(i, i ^ flip) for i in range(size)])]
    reduce_sum x18 -> x2, other arithmetic: 28.6 us -> 3.26 us  [the longest x1 1.9 us: per_device(): own_len = jnp.sum(jnp.where(host_ids == own_block, block_lengths, 0))]
    ppermute x0 -> x18, waiting for transfers between devices: none -> 20.5 us  [swap(): return lax.ppermute(x, axis, [(i, i ^ flip) for i in range(size)])]
    lt x17 -> x0, other arithmetic: 11.6 us -> none  [the longest x9 6.14 us: block_attention(): positions[None, :] < own_len]
    add x14 -> x0, other arithmetic: 8.61 us -> none  [the longest x7 8.49 us: merge_pair(): first[2] * first_factor[..., None] + second[2] * second_factor[..., None]]
  transfers between devices with their start and end apart: 3 -> 18, of which waited for: 1 -> 11; matrix products, arithmetic and copies ran while one was open for 49% -> 7% of each run, Pallas kernels for 0% -> 7%
where the time goes in v1:
time: 110 us; the launch traced here: 108 us
  Pallas kernels  45.5 us (41%)
  starting transfers between devices  26.9 us (24%)
  waiting for transfers between devices  20.5 us (19%)
  other arithmetic  8.37 us (8%)
  between operations  3.81 us (3%)
  local copies, waits for them, and re-layouts  2.69 us (2%)
    pallas_call x1, Pallas kernels, context_attention(): pl.pallas_call(functools.partial(context_kernel, tq=tq, tk=tk, hp=hp, st=...  37.7 us
    ppermute x18, starting transfers between devices, swap(): return lax.ppermute(x, axis, [(i, i ^ flip) for i in range(size)])  26.9 us
    ppermute x18, waiting for transfers between devices, swap(): return lax.ppermute(x, axis, [(i, i ^ flip) for i in range(size)])  20.5 us
    pallas_call x1, Pallas kernels, host_partials(): pl.pallas_call(functools.partial(partial_kernel, hd=hd, step=16, blocks=b...  3.26 us
    unnamed x22, local copies, waits for them, and re-layouts  2.69 us
  transfers between devices with their start and end apart: 18, of which 11 were waited for; matrix products, arithmetic and copies ran while one was open for 7% of the time, Pallas kernels for 7%

profile of v1, /device:TPU:0, one launch (start us, length us, event | category | flops | bytes accessed | tf_op | source)
XLA Modules:
  0.0 107.8 jit_solution(17414508800807729033)
XLA Ops:
  0.6 0.0 copy-start
  0.7 1.1 %broadcast_select_fusion.4 = bf16[1024,128]{1,0:T(8,128)(2,1)S(1)} fusion(bf16[1024,128]{1,0:T(8,128)(2,1)} %refs_5_.1, bf16[1024,128]{1,0:T(8,128)(2,1)} %refs_4_.2, pred[]{:T(512)S(6)} %eq.36), kind=kLoop, calls=%fused_computation.5 | loop fusion | flops 131072 | bytes 786433 | tf_op jit(solution)/shard_map/jit(_where)/select_n | solution.py:302
  1.8 3.0 %collective-permute-start = (bf16[1024,128]{1,0:T(8,128)(2,1)S(1)}, bf16[1024,128]{1,0:T(8,128)(2,1)S(1)}, u32[]{:S(2)}, u32[]{:S(2)}) collective-permute-start(bf16[1024,128]{1,0:T(8,128)(2,1)S(1)} %broadcast_select_fusion.4), channel_id=1, source_target_pairs={{0,4},{4,0},{8,12},{12,8},{16,20},{20,16},{24,28},{28,24},{1,5},{5... | collective-permute-start | bytes 786440 | tf_op jit(solution)/shard_map/ppermute | solution.py:267
  4.9 0.1 collective-permute-start.4
  4.9 1.4 %fusion.2 = (s32[]{:T(128)}, s32[]{:T(128)}) fusion(s32[8]{0:T(128)} %param.12, s32[]{:T(128)S(6)} %axis_index.23), kind=kLoop, calls=%fused_computation.15 | loop fusion | flops 46 | bytes 44 | tf_op jit(solution)/shard_map/reduce_sum | solution.py:286
  7.7 1.9 %fusion.1 = s32[]{:T(128)} fusion(s32[8]{0:T(128)} %param.13, s32[]{:T(128)} %get-tuple-element.19), kind=kLoop, calls=%fused_computation.14 | loop fusion | flops 23 | bytes 40 | tf_op jit(solution)/shard_map/reduce_sum | solution.py:285
  9.6 1.8 %collective-permute-done = bf16[1024,128]{1,0:T(8,128)(2,1)S(1)} collective-permute-done((bf16[1024,128]{1,0:T(8,128)(2,1)S(1)}, bf16[1024,128]{1,0:T(8,128)(2,1)S(1)}, u32[]{:S(2)}, u32[]{:S(2)}) %collective-permute-start) | collective-permute-done | bytes 262176 | tf_op jit(solution)/shard_map/ppermute | solution.py:267
  11.3 1.0 select_select_fusion
  12.3 1.9 %collective-permute-start.1 = (bf16[1024,128]{1,0:T(8,128)(2,1)S(1)}, bf16[1024,128]{1,0:T(8,128)(2,1)S(1)}, u32[]{:S(2)}, u32[]{:S(2)}) collective-permute-start(bf16[1024,128]{1,0:T(8,128)(2,1)S(1)} %select_select_fusion), channel_id=1, source_target_pairs={{0,8},{4,12},{8,0},{12,4},{16,24},{20,28},{24,16},{28,20},{1,9},{5... | collective-permute-start | bytes 786440 | tf_op jit(solution)/shard_map/ppermute | solution.py:267
  14.2 0.7 broadcast_select_fusion.6
  14.9 0.3 collective-permute-start.5
  15.2 2.8 %collective-permute-start.6 = (bf16[16,1024]{1,0:T(8,128)(2,1)S(1)}, bf16[16,1024]{1,0:T(8,128)(2,1)S(1)}, u32[]{:S(2)}, u32[]{:S(2)}) collective-permute-start(bf16[16,1024]{1,0:T(8,128)(2,1)S(1)} %pad_maximum_fusion.refs_0_), channel_id=1, source_target_pairs={{0,16},{4,20},{8,24},{12,28},{16,0},{20,4},{24,8},{28,12},{1,17},{... | collective-permute-start | bytes 98312 | tf_op jit(solution)/shard_map/ppermute | solution.py:267
  18.0 1.3 %collective-permute-start.7 = (bf16[16,1024]{1,0:T(8,128)(2,1)S(1)}, bf16[16,1024]{1,0:T(8,128)(2,1)S(1)}, u32[]{:S(2)}, u32[]{:S(2)}) collective-permute-start(bf16[16,1024]{1,0:T(8,128)(2,1)S(1)} %pad_maximum_fusion.refs_0_), channel_id=1, source_target_pairs={{0,24},{4,28},{8,16},{12,20},{16,8},{20,12},{24,0},{28,4},{1,25},{... | collective-permute-start | bytes 98312 | tf_op jit(solution)/shard_map/ppermute | solution.py:267
  19.4 1.4 %collective-permute-done.1 = bf16[1024,128]{1,0:T(8,128)(2,1)S(1)} collective-permute-done((bf16[1024,128]{1,0:T(8,128)(2,1)S(1)}, bf16[1024,128]{1,0:T(8,128)(2,1)S(1)}, u32[]{:S(2)}, u32[]{:S(2)}) %collective-permute-start.1) | collective-permute-done | bytes 262176 | tf_op jit(solution)/shard_map/ppermute | solution.py:267
  20.8 2.8 %collective-permute-start.2 = (bf16[1024,128]{1,0:T(8,128)(2,1)S(1)}, bf16[1024,128]{1,0:T(8,128)(2,1)S(1)}, u32[]{:S(2)}, u32[]{:S(2)}) collective-permute-start(bf16[1024,128]{1,0:T(8,128)(2,1)S(1)} %broadcast_select_fusion), channel_id=1, source_target_pairs={{0,16},{4,20},{8,24},{12,28},{16,0},{20,4},{24,8},{28,12},{1,17},{... | collective-permute-start | bytes 786440 | tf_op jit(solution)/shard_map/ppermute | solution.py:267
  23.6 0.7 pad_add_fusion.2.scal
  24.3 0.8 collective-permute-done.7.refs_3_
  25.2 3.3 %host_partials.1 = (f32[136,128]{1,0:T(8,128)S(1)}, f32[136,128]{1,0:T(8,128)S(1)}, f32[136,128]{1,0:T(8,128)S(1)}, f32[136,128]{1,0:T(8,128)S(1)}) custom-call(s32[2]{0:T(128)S(1)} %pad_add_fusion.2.scal, bf16[16,1024]{1,0:T(8,128)(2,1)S(1)} %pad_maximum_fusion.refs_0_, bf16[16,1024]{1,0:T(8,128)(2,1)S(1)} %collective-permute-done.5.refs_1_, ...), custom_call_target="tpu_custom_call" | custom-call | tf_op jit(solution)/shard_map/host_partials/pallas_call | solution.py:169
  28.4 0.6 copy-done.4
  29.1 3.3 %collective-permute-start.8 = (f32[136,128]{1,0:T(8,128)S(1)}, f32[136,128]{1,0:T(8,128)S(1)}, u32[]{:S(2)}, u32[]{:S(2)}) collective-permute-start(f32[136,128]{1,0:T(8,128)S(1)} %get-tuple-element.11), channel_id=1, source_target_pairs={{0,8},{4,12},{8,0},{12,4},{16,24},{20,28},{24,16},{28,20},{1,9},{5... | collective-permute-start | bytes 208904 | tf_op jit(solution)/shard_map/ppermute | solution.py:267
  32.4 2.4 %collective-permute-start.10 = (f32[136,128]{1,0:T(8,128)S(1)}, f32[136,128]{1,0:T(8,128)S(1)}, u32[]{:S(2)}, u32[]{:S(2)}) collective-permute-start(f32[136,128]{1,0:T(8,128)S(1)} %get-tuple-element.13), channel_id=1, source_target_pairs={{0,24},{4,28},{8,16},{12,20},{16,8},{20,12},{24,0},{28,4},{1,25},{... | collective-permute-start | bytes 208904 | tf_op jit(solution)/shard_map/ppermute | solution.py:267
  34.8 2.2 %collective-permute-done.8.refs_1_ = f32[136,128]{1,0:T(8,128)S(1)} collective-permute-done((f32[136,128]{1,0:T(8,128)S(1)}, f32[136,128]{1,0:T(8,128)S(1)}, u32[]{:S(2)}, u32[]{:S(2)}) %collective-permute-start.8) | collective-permute-done | bytes 69664 | tf_op jit(solution)/shard_map/ppermute | solution.py:267
  37.0 2.4 %collective-permute-done.9.refs_2_ = f32[136,128]{1,0:T(8,128)S(1)} collective-permute-done((f32[136,128]{1,0:T(8,128)S(1)}, f32[136,128]{1,0:T(8,128)S(1)}, u32[]{:S(2)}, u32[]{:S(2)}) %collective-permute-start.9) | collective-permute-done | bytes 69664 | tf_op jit(solution)/shard_map/ppermute | solution.py:267
  39.4 0.6 copy-done.7
  40.0 0.0 copy-done.8
  40.1 1.6 %merge_partials.1.refs_0_ = f32[136,128]{1,0:T(8,128)} custom-call(f32[136,128]{1,0:T(8,128)} %copy-done.4, f32[136,128]{1,0:T(8,128)} %copy-done.6, f32[136,128]{1,0:T(8,128)} %copy-done.7, f32[136,128]{1,0:T(8,128)} %copy-done.8), custom_call_target="tpu_custom_call" | custom-call | tf_op jit(solution)/shard_map/merge_partials/pallas_call | solution.py:200
  41.7 1.1 %collective-permute-start.11 = (f32[136,128]{1,0:T(8,128)}, f32[136,128]{1,0:T(8,128)S(1)}, u32[]{:S(2)}, u32[]{:S(2)}) collective-permute-start(f32[136,128]{1,0:T(8,128)} %merge_partials.1.refs_0_), channel_id=1, source_target_pairs={{0,4},{4,0},{8,12},{12,8},{16,20},{20,16},{24,28},{28,24},{1,5},{5... | collective-permute-start | bytes 208904 | tf_op jit(solution)/shard_map/ppermute | solution.py:267
  42.8 3.4 %collective-permute-done.11.refs_1_ = f32[136,128]{1,0:T(8,128)S(1)} collective-permute-done((f32[136,128]{1,0:T(8,128)}, f32[136,128]{1,0:T(8,128)S(1)}, u32[]{:S(2)}, u32[]{:S(2)}) %collective-permute-start.11) | collective-permute-done | bytes 69664 | tf_op jit(solution)/shard_map/ppermute | solution.py:267
  46.2 0.6 copy-done.9
  46.8 1.9 %finish_queries.1.refs_0_ = bf16[64,256]{1,0:T(8,128)(2,1)} custom-call(f32[136,128]{1,0:T(8,128)} %merge_partials.1.refs_0_, f32[136,128]{1,0:T(8,128)} %copy-done.9), custom_call_target="tpu_custom_call" | custom-call | tf_op jit(solution)/shard_map/finish_queries/pallas_call | solution.py:226
  48.7 1.3 %collective-permute-start.12 = (bf16[64,256]{1,0:T(8,128)(2,1)}, bf16[64,256]{1,0:T(8,128)(2,1)S(1)}, u32[]{:S(2)}, u32[]{:S(2)}) collective-permute-start(bf16[64,256]{1,0:T(8,128)(2,1)} %finish_queries.1.refs_0_), channel_id=1, source_target_pairs={{0,8},{4,12},{8,0},{12,4},{16,24},{20,28},{24,16},{28,20},{1,9},{5... | collective-permute-start | bytes 98312 | tf_op jit(solution)/shard_map/ppermute | solution.py:267
  50.0 1.5 %collective-permute-start.13 = (bf16[64,256]{1,0:T(8,128)(2,1)}, bf16[64,256]{1,0:T(8,128)(2,1)S(1)}, u32[]{:S(2)}, u32[]{:S(2)}) collective-permute-start(bf16[64,256]{1,0:T(8,128)(2,1)} %finish_queries.1.refs_0_), channel_id=1, source_target_pairs={{0,16},{4,20},{8,24},{12,28},{16,0},{20,4},{24,8},{28,12},{1,17},{... | collective-permute-start | bytes 98312 | tf_op jit(solution)/shard_map/ppermute | solution.py:267
  51.5 1.6 %collective-permute-start.14 = (bf16[64,256]{1,0:T(8,128)(2,1)}, bf16[64,256]{1,0:T(8,128)(2,1)S(1)}, u32[]{:S(2)}, u32[]{:S(2)}) collective-permute-start(bf16[64,256]{1,0:T(8,128)(2,1)} %finish_queries.1.refs_0_), channel_id=1, source_target_pairs={{0,24},{4,28},{8,16},{12,20},{16,8},{20,12},{24,0},{28,4},{1,25},{... | collective-permute-start | bytes 98312 | tf_op jit(solution)/shard_map/ppermute | solution.py:267
  53.1 0.1 pad_add_fusion.1.scal
  54.5 0.9 collective-permute-done.13.refs_2_
  55.4 2.0 %collective-permute-done.14.refs_3_ = bf16[64,256]{1,0:T(8,128)(2,1)S(1)} collective-permute-done((bf16[64,256]{1,0:T(8,128)(2,1)}, bf16[64,256]{1,0:T(8,128)(2,1)S(1)}, u32[]{:S(2)}, u32[]{:S(2)}) %collective-permute-start.14) | collective-permute-done | bytes 32800 | tf_op jit(solution)/shard_map/ppermute | solution.py:267
  57.4 0.8 copy-done.3
  58.2 1.0 project.1
  59.2 0.1 collective-permute-start.17
  59.3 1.6 %collective-permute-start.16 = (f32[16,1024]{1,0:T(8,128)S(1)}, f32[16,1024]{1,0:T(8,128)S(1)}, u32[]{:S(2)}, u32[]{:S(2)}) collective-permute-start(f32[16,1024]{1,0:T(8,128)S(1)} %get-tuple-element.16), channel_id=1, source_target_pairs={{0,2},{1,3},{2,0},{3,1},{4,6},{5,7},{6,4},{7,5},{8,10},{9,11},{10,... | collective-permute-start | bytes 196616 | tf_op jit(solution)/shard_map/ppermute | solution.py:267
  60.9 0.3 collective-permute-start.15
  61.2 1.6 %collective-permute-start.3 = (bf16[1024,128]{1,0:T(8,128)(2,1)S(1)}, bf16[1024,128]{1,0:T(8,128)(2,1)S(1)}, u32[]{:S(2)}, u32[]{:S(2)}) collective-permute-start(bf16[1024,128]{1,0:T(8,128)(2,1)S(1)} %broadcast_select_fusion.1), channel_id=1, source_target_pairs={{0,4},{4,0},{8,12},{12,8},{16,20},{20,16},{24,28},{28,24},{1,5},{5... | collective-permute-start | bytes 786440 | tf_op jit(solution)/shard_map/ppermute | solution.py:267
  62.8 0.7 pad_add_fusion.lens
  63.5 0.1 collective-permute-done.17
  63.6 1.5 %collective-permute-done.16 = f32[16,1024]{1,0:T(8,128)S(1)} collective-permute-done((f32[16,1024]{1,0:T(8,128)S(1)}, f32[16,1024]{1,0:T(8,128)S(1)}, u32[]{:S(2)}, u32[]{:S(2)}) %collective-permute-start.16) | collective-permute-done | bytes 65568 | tf_op jit(solution)/shard_map/ppermute | solution.py:267
  65.1 0.6 add_convert_fusion
  65.7 4.0 %collective-permute-done.3 = bf16[1024,128]{1,0:T(8,128)(2,1)S(1)} collective-permute-done((bf16[1024,128]{1,0:T(8,128)(2,1)S(1)}, bf16[1024,128]{1,0:T(8,128)(2,1)S(1)}, u32[]{:S(2)}, u32[]{:S(2)}) %collective-permute-start.3) | collective-permute-done | bytes 262176 | tf_op jit(solution)/shard_map/ppermute | solution.py:267
  69.7 37.7 %context_attention.1 = bf16[1024,1024]{1,0:T(8,128)(2,1)} custom-call(s32[3]{0:T(128)S(1)} %pad_add_fusion.lens, bf16[1024,1024]{1,0:T(8,128)(2,1)S(1)} %copy-done.5, bf16[1024,128]{1,0:T(8,128)(2,1)S(1)} %copy-done, bf16[1024,128]{1,0:T(8,128)(2,1)S(1)} %copy-done.1, bf16[1024,128]{1,0:T(8,128)(2,1)S(1)} %get-tuple-element.21.ak_ref, ...), custom_call_target="tpu_custom_call" | custom-call | flops 6442450944 | bytes 5242880 | tf_op jit(solution)/shard_map/context_attention/pallas_call | solution.py:100
  (28 shorter events, 0.2 us)
Async XLA Ops:
  0.6 24.5 %copy-start = (bf16[1024,128]{1,0:T(8,128)(2,1)S(1)}, bf16[1024,128]{1,0:T(8,128)(2,1)}, u32[]{:S(2)}) copy-start(bf16[1024,128]{1,0:T(8,128)(2,1)} %refs_4_.2) | copy-start | bytes 786436
  0.6 24.5 %copy-start.1 = (bf16[1024,128]{1,0:T(8,128)(2,1)S(1)}, bf16[1024,128]{1,0:T(8,128)(2,1)}, u32[]{:S(2)}) copy-start(bf16[1024,128]{1,0:T(8,128)(2,1)} %refs_5_.1) | copy-start | bytes 786436
  0.7 53.1 %copy-start.10 = (s32[8]{0:T(128)S(1)}, s32[8]{0:T(128)}, u32[]{:S(2)}) copy-start(s32[8]{0:T(128)} %param.13) | copy-start | bytes 100
  0.7 56.7 %copy-start.2 = (bf16[1024,1024]{1,0:T(8,128)(2,1)S(1)}, bf16[1024,1024]{1,0:T(8,128)(2,1)}, u32[]{:S(2)}) copy-start(bf16[1024,1024]{1,0:T(8,128)(2,1)} %refs_4_.3) | copy-start | bytes 6291460
  1.8 9.5 %collective-permute-start = (bf16[1024,128]{1,0:T(8,128)(2,1)S(1)}, bf16[1024,128]{1,0:T(8,128)(2,1)S(1)}, u32[]{:S(2)}, u32[]{:S(2)}) collective-permute-start(bf16[1024,128]{1,0:T(8,128)(2,1)S(1)} %broadcast_select_fusion.4), channel_id=1, source_target_pairs={{0,4},{4,0},{8,12},{12,8},{16,20},{20,16},{24,28},{28,24},{1,5},{5... | collective-permute-start | bytes 786440 | tf_op jit(solution)/shard_map/ppermute | solution.py:267
  4.9 9.3 %collective-permute-start.4 = (bf16[8,1024]{1,0:T(8,128)(2,1)}, bf16[8,1024]{1,0:T(8,128)(2,1)S(1)}, u32[]{:S(2)}, u32[]{:S(2)}) collective-permute-start(bf16[8,1024]{1,0:T(8,128)(2,1)} %param.10), channel_id=1, source_target_pairs={{0,4},{4,0},{8,12},{12,8},{16,20},{20,16},{24,28},{28,24},{1,5},{5... | collective-permute-start | bytes 49160 | tf_op jit(solution)/shard_map/ppermute | solution.py:267
  12.3 8.4 %collective-permute-start.1 = (bf16[1024,128]{1,0:T(8,128)(2,1)S(1)}, bf16[1024,128]{1,0:T(8,128)(2,1)S(1)}, u32[]{:S(2)}, u32[]{:S(2)}) collective-permute-start(bf16[1024,128]{1,0:T(8,128)(2,1)S(1)} %select_select_fusion), channel_id=1, source_target_pairs={{0,8},{4,12},{8,0},{12,4},{16,24},{20,28},{24,16},{28,20},{1,9},{5... | collective-permute-start | bytes 786440 | tf_op jit(solution)/shard_map/ppermute | solution.py:267
  14.9 9.4 %collective-permute-start.5 = (bf16[16,1024]{1,0:T(8,128)(2,1)S(1)}, bf16[16,1024]{1,0:T(8,128)(2,1)S(1)}, u32[]{:S(2)}, u32[]{:S(2)}) collective-permute-start(bf16[16,1024]{1,0:T(8,128)(2,1)S(1)} %pad_maximum_fusion.refs_0_), channel_id=1, source_target_pairs={{0,8},{4,12},{8,0},{12,4},{16,24},{20,28},{24,16},{28,20},{1,9},{5... | collective-permute-start | bytes 98312 | tf_op jit(solution)/shard_map/ppermute | solution.py:267
  15.2 9.1 %collective-permute-start.6 = (bf16[16,1024]{1,0:T(8,128)(2,1)S(1)}, bf16[16,1024]{1,0:T(8,128)(2,1)S(1)}, u32[]{:S(2)}, u32[]{:S(2)}) collective-permute-start(bf16[16,1024]{1,0:T(8,128)(2,1)S(1)} %pad_maximum_fusion.refs_0_), channel_id=1, source_target_pairs={{0,16},{4,20},{8,24},{12,28},{16,0},{20,4},{24,8},{28,12},{1,17},{... | collective-permute-start | bytes 98312 | tf_op jit(solution)/shard_map/ppermute | solution.py:267
  18.0 7.1 %collective-permute-start.7 = (bf16[16,1024]{1,0:T(8,128)(2,1)S(1)}, bf16[16,1024]{1,0:T(8,128)(2,1)S(1)}, u32[]{:S(2)}, u32[]{:S(2)}) collective-permute-start(bf16[16,1024]{1,0:T(8,128)(2,1)S(1)} %pad_maximum_fusion.refs_0_), channel_id=1, source_target_pairs={{0,24},{4,28},{8,16},{12,20},{16,8},{20,12},{24,0},{28,4},{1,25},{... | collective-permute-start | bytes 98312 | tf_op jit(solution)/shard_map/ppermute | solution.py:267
  20.8 40.3 %collective-permute-start.2 = (bf16[1024,128]{1,0:T(8,128)(2,1)S(1)}, bf16[1024,128]{1,0:T(8,128)(2,1)S(1)}, u32[]{:S(2)}, u32[]{:S(2)}) collective-permute-start(bf16[1024,128]{1,0:T(8,128)(2,1)S(1)} %broadcast_select_fusion), channel_id=1, source_target_pairs={{0,16},{4,20},{8,24},{12,28},{16,0},{20,4},{24,8},{28,12},{1,17},{... | collective-permute-start | bytes 786440 | tf_op jit(solution)/shard_map/ppermute | solution.py:267
  28.4 0.6 copy-start.4
  29.1 7.9 %collective-permute-start.8 = (f32[136,128]{1,0:T(8,128)S(1)}, f32[136,128]{1,0:T(8,128)S(1)}, u32[]{:S(2)}, u32[]{:S(2)}) collective-permute-start(f32[136,128]{1,0:T(8,128)S(1)} %get-tuple-element.11), channel_id=1, source_target_pairs={{0,8},{4,12},{8,0},{12,4},{16,24},{20,28},{24,16},{28,20},{1,9},{5... | collective-permute-start | bytes 208904 | tf_op jit(solution)/shard_map/ppermute | solution.py:267
  32.4 7.0 %collective-permute-start.9 = (f32[136,128]{1,0:T(8,128)S(1)}, f32[136,128]{1,0:T(8,128)S(1)}, u32[]{:S(2)}, u32[]{:S(2)}) collective-permute-start(f32[136,128]{1,0:T(8,128)S(1)} %get-tuple-element.12), channel_id=1, source_target_pairs={{0,16},{4,20},{8,24},{12,28},{16,0},{20,4},{24,8},{28,12},{1,17},{... | collective-permute-start | bytes 208904 | tf_op jit(solution)/shard_map/ppermute | solution.py:267
  32.4 7.0 %collective-permute-start.10 = (f32[136,128]{1,0:T(8,128)S(1)}, f32[136,128]{1,0:T(8,128)S(1)}, u32[]{:S(2)}, u32[]{:S(2)}) collective-permute-start(f32[136,128]{1,0:T(8,128)S(1)} %get-tuple-element.13), channel_id=1, source_target_pairs={{0,24},{4,28},{8,16},{12,20},{16,8},{20,12},{24,0},{28,4},{1,25},{... | collective-permute-start | bytes 208904 | tf_op jit(solution)/shard_map/ppermute | solution.py:267
  37.0 2.4 %copy-start.6 = (f32[136,128]{1,0:T(8,128)}, f32[136,128]{1,0:T(8,128)S(1)}, u32[]{:S(2)}) copy-start(f32[136,128]{1,0:T(8,128)S(1)} %collective-permute-done.8.refs_1_) | copy-start | bytes 208900
  39.4 0.6 copy-start.7
  39.4 0.6 copy-start.8
  41.7 4.5 %collective-permute-start.11 = (f32[136,128]{1,0:T(8,128)}, f32[136,128]{1,0:T(8,128)S(1)}, u32[]{:S(2)}, u32[]{:S(2)}) collective-permute-start(f32[136,128]{1,0:T(8,128)} %merge_partials.1.refs_0_), channel_id=1, source_target_pairs={{0,4},{4,0},{8,12},{12,8},{16,20},{20,16},{24,28},{28,24},{1,5},{5... | collective-permute-start | bytes 208904 | tf_op jit(solution)/shard_map/ppermute | solution.py:267
  46.2 0.6 copy-start.9
  48.7 5.8 %collective-permute-start.12 = (bf16[64,256]{1,0:T(8,128)(2,1)}, bf16[64,256]{1,0:T(8,128)(2,1)S(1)}, u32[]{:S(2)}, u32[]{:S(2)}) collective-permute-start(bf16[64,256]{1,0:T(8,128)(2,1)} %finish_queries.1.refs_0_), channel_id=1, source_target_pairs={{0,8},{4,12},{8,0},{12,4},{16,24},{20,28},{24,16},{28,20},{1,9},{5... | collective-permute-start | bytes 98312 | tf_op jit(solution)/shard_map/ppermute | solution.py:267
  50.0 5.4 %collective-permute-start.13 = (bf16[64,256]{1,0:T(8,128)(2,1)}, bf16[64,256]{1,0:T(8,128)(2,1)S(1)}, u32[]{:S(2)}, u32[]{:S(2)}) collective-permute-start(bf16[64,256]{1,0:T(8,128)(2,1)} %finish_queries.1.refs_0_), channel_id=1, source_target_pairs={{0,16},{4,20},{8,24},{12,28},{16,0},{20,4},{24,8},{28,12},{1,17},{... | collective-permute-start | bytes 98312 | tf_op jit(solution)/shard_map/ppermute | solution.py:267
  51.5 5.9 %collective-permute-start.14 = (bf16[64,256]{1,0:T(8,128)(2,1)}, bf16[64,256]{1,0:T(8,128)(2,1)S(1)}, u32[]{:S(2)}, u32[]{:S(2)}) collective-permute-start(bf16[64,256]{1,0:T(8,128)(2,1)} %finish_queries.1.refs_0_), channel_id=1, source_target_pairs={{0,24},{4,28},{8,16},{12,20},{16,8},{20,12},{24,0},{28,4},{1,25},{... | collective-permute-start | bytes 98312 | tf_op jit(solution)/shard_map/ppermute | solution.py:267
  57.4 0.8 copy-start.3
  58.2 11.6 %copy-start.5 = (bf16[1024,1024]{1,0:T(8,128)(2,1)S(1)}, bf16[1024,1024]{1,0:T(8,128)(2,1)}, u32[]{:S(2)}) copy-start(bf16[1024,1024]{1,0:T(8,128)(2,1)} %q_ref.1) | copy-start | bytes 6291460
  59.2 4.4 %collective-permute-start.17 = (f32[16,1024]{1,0:T(8,128)S(1)}, f32[16,1024]{1,0:T(8,128)S(1)}, u32[]{:S(2)}, u32[]{:S(2)}) collective-permute-start(f32[16,1024]{1,0:T(8,128)S(1)} %get-tuple-element.17), channel_id=1, source_target_pairs={{0,3},{1,2},{2,1},{3,0},{4,7},{5,6},{6,5},{7,4},{8,11},{9,10},{10,... | collective-permute-start | bytes 196616 | tf_op jit(solution)/shard_map/ppermute | solution.py:267
  59.3 5.8 %collective-permute-start.16 = (f32[16,1024]{1,0:T(8,128)S(1)}, f32[16,1024]{1,0:T(8,128)S(1)}, u32[]{:S(2)}, u32[]{:S(2)}) collective-permute-start(f32[16,1024]{1,0:T(8,128)S(1)} %get-tuple-element.16), channel_id=1, source_target_pairs={{0,2},{1,3},{2,0},{3,1},{4,6},{5,7},{6,4},{7,5},{8,10},{9,11},{10,... | collective-permute-start | bytes 196616 | tf_op jit(solution)/shard_map/ppermute | solution.py:267
  60.9 4.2 %collective-permute-start.15 = (f32[16,1024]{1,0:T(8,128)S(1)}, f32[16,1024]{1,0:T(8,128)S(1)}, u32[]{:S(2)}, u32[]{:S(2)}) collective-permute-start(f32[16,1024]{1,0:T(8,128)S(1)} %get-tuple-element.15), channel_id=1, source_target_pairs={{0,1},{1,0},{2,3},{3,2},{4,5},{5,4},{6,7},{7,6},{8,9},{9,8},{10,11... | collective-permute-start | bytes 196616 | tf_op jit(solution)/shard_map/ppermute | solution.py:267
  61.2 8.5 %collective-permute-start.3 = (bf16[1024,128]{1,0:T(8,128)(2,1)S(1)}, bf16[1024,128]{1,0:T(8,128)(2,1)S(1)}, u32[]{:S(2)}, u32[]{:S(2)}) collective-permute-start(bf16[1024,128]{1,0:T(8,128)(2,1)S(1)} %broadcast_select_fusion.1), channel_id=1, source_target_pairs={{0,4},{4,0},{8,12},{12,8},{16,20},{20,16},{24,28},{28,24},{1,5},{5... | collective-permute-start | bytes 786440 | tf_op jit(solution)/shard_map/ppermute | solution.py:267
